TPU v7x, 32 devices: a whole 2x2x4 slice. The times are simulated.
32 devices in a mesh: groups: 2 (over y), row: 4 (over x, core), col: 4 (over z).
Axes of the slice: x: 2, y: 2, z: 4, core: 2. Of those that a mesh axis runs over, the one named last changes fastest.
Arguments:
- pair_rep: float32 [256, 128, 128], P(('groups', 'row'), 'col'), parts along dimension 0, may hold values from -6 to 6
- chain_ids: int32 [256], P('groups'), parts along dimension 0, may hold values from 0 to 5, never falling along the last dimension, each value on 1 to 64 neighbouring positions
- residue_mask: int32 [256], P('groups'), parts along dimension 0, may hold values from 0 to 1, as said below
- norm_gain: float32 [128], replicated, may hold values from 0.1 to 1.9
- norm_bias: float32 [128], replicated, may hold values from -3 to 3
- chain_bias: float32 [128], replicated, may hold values from -4 to 4
- proj_in: bfloat16 [128, 640], replicated, may hold values from -0.5 to 0.5
- out_gain: float32 [128], replicated, may hold values from 0.1 to 1.9
- out_bias: float32 [128], replicated, may hold values from -3 to 3
- proj_out: bfloat16 [128, 128], replicated, may hold values from -0.5 to 0.5
Outputs:
- pair_next: float32 [256, 128, 128], P(('groups', 'row'), 'col'), parts along dimension 0
There are 2 independent parts, one for each index of `groups`. A program takes and returns all parts, laid end to end along the dimension named above; an argument that names none is the same for every part. Nothing has to cross between parts.
Inputs may be any that keep to these rules, and one draw needn't show every extreme that they name: `chain_ids`: chain numbers never decrease along the residues, and every chain number appears. `residue_mask`: the residues below a length of at least 64 and below 128 are 1, all later ones 0.
All inputs are finite; a program needn't handle non-finite values.
Results may differ from a plain program's by a relative error of at most 0.0021.
Values may be sent and summed in bfloat16 or wider, within the bound.
A program may use at most 128 MiB of HBM per device.

v0:
```python
import jax
import jax.numpy as jnp
from jax import lax
from jax.sharding import PartitionSpec as P

C = 128


def broadcast(block, axis, owner):
    block = jnp.where(lax.axis_index(axis) == owner, block, jnp.zeros_like(block))
    return lax.psum(block, axis)


def layer_norm(values, gain, bias):
    center = values - jnp.mean(values, axis=-1, keepdims=True)
    variance = jnp.mean(center * center, axis=-1, keepdims=True)
    return center * lax.rsqrt(variance + 1e-05) * gain + bias


def per_device(
    pair_rep,
    chain_ids,
    residue_mask,
    norm_gain,
    norm_bias,
    chain_bias,
    proj_in,
    out_gain,
    out_bias,
    proj_out,
):
    row_count = pair_rep.shape[0]
    col_count = pair_rep.shape[1]
    row_index = lax.axis_index("row")
    col_index = lax.axis_index("col")
    chain_rows = lax.dynamic_slice_in_dim(chain_ids, row_index * row_count, row_count)
    chain_cols = lax.dynamic_slice_in_dim(chain_ids, col_index * col_count, col_count)
    live_rows = lax.dynamic_slice_in_dim(residue_mask, row_index * row_count, row_count).astype(
        jnp.float32
    )
    live_cols = lax.dynamic_slice_in_dim(residue_mask, col_index * col_count, col_count).astype(
        jnp.float32
    )
    same_chain = (chain_rows[:, None] == chain_cols[None, :]).astype(jnp.float32)
    pair_in = pair_rep + same_chain[:, :, None] * chain_bias
    normed = layer_norm(pair_in, norm_gain, norm_bias).astype(jnp.bfloat16)
    projected = jnp.dot(normed.reshape(-1, C), proj_in, preferred_element_type=jnp.float32)
    projected = projected.reshape(row_count, col_count, 5 * C)
    pair_mask = (live_rows[:, None] * live_cols[None, :])[:, :, None]
    left = (jax.nn.sigmoid(projected[:, :, 0:C]) * projected[:, :, C : 2 * C] * pair_mask).astype(
        jnp.bfloat16
    )
    right = (
        jax.nn.sigmoid(projected[:, :, 2 * C : 3 * C]) * projected[:, :, 3 * C : 4 * C] * pair_mask
    ).astype(jnp.bfloat16)
    gate_vals = jax.nn.sigmoid(projected[:, :, 4 * C : 5 * C])
    fine_ratio = lax.axis_size("col") // lax.axis_size("row")
    whole_row = lax.all_gather(right, "col", axis=1, tiled=True)
    wanted = col_index % fine_ratio * col_count
    own_part = lax.dynamic_slice_in_dim(whole_row, wanted, col_count, 0)
    right_t = broadcast(own_part, "row", col_index // fine_ratio)
    mixed = jnp.einsum(
        "ikc,jkc->ijc",
        lax.all_gather(left, "col", axis=1, tiled=True),
        right_t,
        preferred_element_type=jnp.float32,
    )
    mixed_norm = layer_norm(mixed, out_gain, out_bias).astype(jnp.bfloat16)
    update = jnp.dot(mixed_norm.reshape(-1, C), proj_out, preferred_element_type=jnp.float32)
    return pair_rep + gate_vals * update.reshape(row_count, col_count, C)


def solution(mesh):
    return jax.shard_map(
        per_device,
        mesh=mesh,
        in_specs=(
            P(("groups", "row"), "col", None),
            P("groups"),
            P("groups"),
            P(),
            P(),
            P(),
            P(),
            P(),
            P(),
            P(),
        ),
        out_specs=P(("groups", "row"), "col", None),
        check_vma=False,
    )
```

profile of v0, /device:TPU:24, one launch (start us, length us, event | category | flops | bytes accessed | tf_op | source)
XLA Modules:
  0.0 129.7 jit_solution(5010411654700681036)
XLA Ops:
  6.5 0.0 copy-start
  6.5 0.0 all-gather.3.cloned.1.call-start
  6.5 0.8 dynamic-slice_convert_fusion.1
  7.4 0.1 compare_convert_fusion
  7.4 1.4 %fusion.14 = f32[32,32]{1,0:T(8,128)S(1)} fusion(f32[32,32,128]{2,1,0:T(8,128)} %param.10, f32[128]{0:T(128)} %param.15, f32[32,32]{1,0:T(8,128)S(1)} %compare_convert_fusion), kind=kLoop, calls=%fused_computation.28 | loop fusion | flops 392192 | bytes 532992 | tf_op jit(solution)/shard_map/reduce_sum | solution.py:15
  8.9 1.5 %multiply_reduce_fusion.1 = f32[32,32]{1,0:T(8,128)S(1)} fusion(f32[32,32,128]{2,1,0:T(8,128)} %param.10, f32[32,32]{1,0:T(8,128)S(1)} %broadcast_multiply_fusion.2, f32[128]{0:T(128)} %param.15, f32[32,32]{1,0:T(8,128)S(1)} %compare_convert_fusion), kind=kLoop, calls=%fused_computation.26 | loop fusion | flops 654336 | bytes 537088 | tf_op jit(solution)/shard_map/reduce_sum | solution.py:16
  10.4 0.1 broadcast_multiply_fusion
  10.5 0.0 copy-done
  10.5 1.8 %fusion.15 = f32[32,32,640]{2,1,0:T(8,128)S(1)} fusion(f32[32,32,128]{2,1,0:T(8,128)} %param.10, f32[128]{0:T(128)} %param.14, f32[128]{0:T(128)} %param.13, f32[32,32]{1,0:T(8,128)S(1)} %add_rsqrt_fusion.1, f32[32,32]{1,0:T(8,128)S(1)} %broadcast_multiply_fusion.2, f32[128]{0:T(128)} %param.15, f32[32,32]{1,0:T(8,128)S(1)} %compare_convert_fusion, ...), kind=kOutput, calls=%fused_computation.29 | convolution fusion | flops 168689664 | bytes 3323392 | tf_op jit(solution)/shard_map/dot_general | solution.py:47
  12.3 1.1 fusion.2
  13.4 0.0 all-gather.3.cloned.1.call-update
  13.4 0.0 all-gather.5.cloned.1.call-start
  13.5 0.7 all-gather.5.cloned.1.call-update
  14.2 0.0 all-reduce.2.cloned.1.call-start
  14.2 26.8 %all-gather.3.cloned.1.call-done = bf16[32,128,128]{2,1,0:T(8,128)(2,1)} async-done(((bf16[32,32,128]{2,1,0:T(8,128)(2,1)}), bf16[32,128,128]{2,1,0:T(8,128)(2,1)}) %all-gather.3.cloned.1.call-update) | async-done | bytes 1048592 | tf_op jit(solution)/shard_map/all_gather | solution.py:58
  41.1 1.0 broadcast_select_fusion
  42.1 0.0 all-reduce.2.cloned.1.call-update
  42.2 28.0 %all-gather.5.cloned.1.call-done = bf16[32,128,128]{2,1,0:T(8,128)(2,1)} async-done(((bf16[32,32,128]{2,1,0:T(8,128)(2,1)}), bf16[32,128,128]{2,1,0:T(8,128)(2,1)}) %all-gather.5.cloned.1.call-update) | async-done | bytes 1048592 | tf_op jit(solution)/shard_map/all_gather | solution.py:64
  70.1 2.7 %copy.29 = bf16[32,128,128]{1,0,2:T(8,128)(2,1)} copy(bf16[32,128,128]{2,1,0:T(8,128)(2,1)} %all-gather.5.cloned.1.call-done) | data formatting | bytes 2097152 | tf_op jit(solution)/shard_map/all_gather | solution.py:64
  72.8 36.7 %all-reduce.2.cloned.1.call-done = bf16[32,128,128]{2,1,0:T(8,128)(2,1)} async-done(((bf16[32,128,128]{2,1,0:T(8,128)(2,1)}), bf16[32,128,128]{2,1,0:T(8,128)(2,1)}) %all-reduce.2.cloned.1.call-update) | async-done | bytes 1048592 | tf_op jit(solution)/shard_map/psum | solution.py:11
  109.5 2.7 %copy.28 = bf16[32,128,128]{1,0,2:T(8,128)(2,1)} copy(bf16[32,128,128]{2,1,0:T(8,128)(2,1)} %all-reduce.2.cloned.1.call-done) | data formatting | bytes 2097152 | tf_op jit(solution)/shard_map/psum | solution.py:11
  112.1 3.5 %bitcast_reduce_fusion = (f32[32,32]{0,1:T(8,128)S(1)}, f32[128,32,32]{2,1,0:T(8,128)}) fusion(bf16[32,128,128]{1,0,2:T(8,128)(2,1)} %copy.28, bf16[32,128,128]{1,0,2:T(8,128)(2,1)} %copy.29), kind=kOutput, calls=%fused_computation | convolution fusion | flops 33684480 | bytes 2625536 | tf_op jit(solution)/shard_map/ikc,jkc->ijc/dot_general | solution.py:62
  115.7 0.0 copy-start.1
  115.7 0.0 copy-start.2
  115.7 0.0 copy-start.3
  115.7 0.0 copy-start.4
  115.7 0.1 copy.32
  115.8 3.6 %copy.30 = f32[128,32,32]{0,1,2:T(8,128)} copy(f32[128,32,32]{2,1,0:T(8,128)} %get-tuple-element.12) | data formatting | bytes 1048576 | tf_op jit(solution)/shard_map/ikc,jkc->ijc/dot_general | solution.py:62
  119.4 1.4 %multiply_reduce_fusion = f32[32,32]{1,0:T(8,128)S(1)} fusion(f32[128,32,32]{0,1,2:T(8,128)} %copy.30, f32[32,32]{1,0:T(8,128)S(1)} %broadcast_multiply_fusion.1), kind=kLoop, calls=%fused_computation.24 | loop fusion | flops 392192 | bytes 532480 | tf_op jit(solution)/shard_map/reduce_sum | solution.py:16
  120.9 0.0 copy-done.1
  120.9 0.0 copy-done.2
  120.9 0.0 copy-done.3
  120.9 0.0 copy-done.4
  120.9 2.3 %fusion = f32[32,32,128]{2,1,0:T(8,128)} fusion(f32[32,32,128]{2,1,0:T(8,128)S(1)} %copy-done.1, f32[32,32,640]{2,1,0:T(8,128)S(1)} %fusion.15, f32[128,32,32]{0,1,2:T(8,128)} %copy.30, f32[128]{0:T(128)S(1)} %copy-done.3, f32[128]{0:T(128)S(1)} %copy-done.4, f32[32,32]{1,0:T(8,128)S(1)} %add_rsqrt_fusion, f32[32,32]{1,0:T(8,128)S(1)} %broadcast_multiply_fusion.1, ...), kind=kOutput, calls=%fused_computation.2 | convolution fusion | flops 34865152 | bytes 2139136 | tf_op jit(solution)/shard_map/dot_general | solution.py:69
  (4 shorter events, 0.0 us)
Async XLA Ops:
  6.5 4.0 %copy-start = (bf16[128,640]{1,0:T(8,128)(2,1)S(1)}, bf16[128,640]{1,0:T(8,128)(2,1)}, u32[]{:S(2)}) copy-start(bf16[128,640]{1,0:T(8,128)(2,1)} %param.16) | copy-start | bytes 491524
  6.5 34.5 %all-gather.3.cloned.1.call-start = ((), (), s32[]{:S(2)}) async-start(), calls=%async_computation | async-start | bytes 1310720 | tf_op jit(solution)/shard_map/all_gather | solution.py:58
  13.4 56.7 %all-gather.5.cloned.1.call-start = ((), (), s32[]{:S(2)}) async-start(), calls=%async_computation.2 | async-start | bytes 1310720 | tf_op jit(solution)/shard_map/all_gather | solution.py:64
  14.2 95.3 %all-reduce.2.cloned.1.call-start = ((), (), s32[]{:S(2)}) async-start(), calls=%async_computation.1 | async-start | bytes 2097152 | tf_op jit(solution)/shard_map/psum | solution.py:11
  115.7 5.2 %copy-start.1 = (f32[32,32,128]{2,1,0:T(8,128)S(1)}, f32[32,32,128]{2,1,0:T(8,128)}, u32[]{:S(2)}) copy-start(f32[32,32,128]{2,1,0:T(8,128)} %param.10) | copy-start | bytes 1572868
  115.7 5.2 %copy-start.2 = (bf16[128,128]{1,0:T(8,128)(2,1)S(1)}, bf16[128,128]{1,0:T(8,128)(2,1)}, u32[]{:S(2)}) copy-start(bf16[128,128]{1,0:T(8,128)(2,1)} %param.19) | copy-start | bytes 98308
  115.7 5.2 %copy-start.3 = (f32[128]{0:T(128)S(1)}, f32[128]{0:T(128)}, u32[]{:S(2)}) copy-start(f32[128]{0:T(128)} %param.18) | copy-start | bytes 1540
  115.7 5.2 %copy-start.4 = (f32[128]{0:T(128)S(1)}, f32[128]{0:T(128)}, u32[]{:S(2)}) copy-start(f32[128]{0:T(128)} %param.17) | copy-start | bytes 1540
Sparse Core Ops, SparseCore 0:
  13.6 27.4 all-gather.2
  42.7 27.4 all-gather.4
  72.5 36.9 all-reduce.1
where the time goes:
time: 132 us; the launch traced here: 130 us
  waiting for transfers between devices  92.2 us (70%)
  between operations  13.2 us (10%)
  local copies, waits for them, and re-layouts  9.07 us (7%)
  matrix products  7.64 us (6%)
  other arithmetic  7.53 us (6%)
    psum x1, waiting for transfers between devices, broadcast(): return lax.psum(block, axis)  36.7 us
    all_gather x1, waiting for transfers between devices, per_device(): lax.all_gather(left, 'col', axis=1, tiled=True)  28 us
    all_gather x1, waiting for transfers between devices, per_device(): whole_row = lax.all_gather(right, 'col', axis=1, tiled=True)  26.8 us
    dot_general x1, local copies, waits for them, and re-layouts, per_device(): jnp.einsum('ikc,jkc->ijc', lax.all_gather(left, 'col', axis=1, tiled=True...  3.63 us
    dot_general x1, matrix products, per_device(): jnp.einsum('ikc,jkc->ijc', lax.all_gather(left, 'col', axis=1, tiled=True...  3.55 us
    reduce_sum x2, other arithmetic, layer_norm(): variance = jnp.mean(center * center, axis=-1, keepdims=True)  2.96 us
    all_gather x1, local copies, waits for them, and re-layouts, per_device(): lax.all_gather(left, 'col', axis=1, tiled=True)  2.68 us
    psum x1, local copies, waits for them, and re-layouts, broadcast(): return lax.psum(block, axis)  2.67 us
  transfers between devices with their start and end apart: 3, of which 3 were waited for; matrix products, arithmetic and copies ran while one was open for 3% of the time, Pallas kernels for 0%

commit v1 on v0

v1 whole, which is shorter than its diff:
```python
import functools

import jax
import jax.numpy as jnp
from jax import lax
from jax.experimental import pallas as pl
from jax.experimental.pallas import tpu as pltpu
from jax.sharding import PartitionSpec as P

C = 128
G = 8
J = 16
F32 = jnp.float32
BF16 = jnp.bfloat16


def layer_norm(values, gain, bias):
    center = values - jnp.mean(values, axis=-1, keepdims=True)
    variance = jnp.mean(center * center, axis=-1, keepdims=True)
    return center * lax.rsqrt(variance + 1e-05) * gain + bias


def as_rows(ref, offset, count):
    shape = (count, ref.shape[1])
    lane = lax.broadcasted_iota(jnp.int32, shape, 1)
    row = lax.broadcasted_iota(jnp.int32, shape, 0)
    values = jnp.broadcast_to(ref[...].astype(F32), shape)
    picked = jnp.sum(jnp.where(lane == row + offset, values, 0.0), axis=1, keepdims=True)
    return jnp.broadcast_to(picked, (count, C))


def kernel(
    R,
    N,
    pair_ref,
    chain_ref,
    mask_ref,
    gain_ref,
    bias_ref,
    chain_bias_ref,
    w_in_ref,
    out_gain_ref,
    out_bias_ref,
    w_out_ref,
    out_ref,
    row_chain,
    col_chain,
    row_live,
    col_live,
    normed,
    left,
    right,
    right_k,
    rights,
    own,
    outbox,
    inbox,
    direct_send,
    core_send,
    right_recv,
    sum_send,
    sum_recv,
):
    rows, cols, _ = pair_ref.shape
    chunks = rows // J
    parts = cols // J
    r = lax.axis_index("row")
    c = lax.axis_index("col")
    sibling = r + 1 - 2 * lax.rem(r, 2)
    half = R // 2

    barrier = pltpu.get_barrier_semaphore()
    pl.semaphore_signal(barrier, inc=1, device_id={"row": sibling})
    for d in range(1, half):
        pl.semaphore_signal(barrier, inc=1, device_id={"row": lax.rem(r + 2 * d, R)})
    for d in range(1, N):
        pl.semaphore_signal(barrier, inc=1, device_id={"col": lax.rem(c + d, N)})

    row_chain[...] = as_rows(chain_ref, r * rows, rows)
    col_chain[...] = as_rows(chain_ref, c * cols, cols)
    row_live[...] = as_rows(mask_ref, r * rows, rows)
    col_live[...] = as_rows(mask_ref, c * cols, cols)

    def direct_copy(d, q):
        return pltpu.make_async_remote_copy(
            src_ref=rights.at[r, q],
            dst_ref=rights.at[r, q],
            send_sem=direct_send.at[d, q],
            recv_sem=right_recv.at[r, q],
            device_id={"row": lax.rem(r + 2 * d, R)},
        )

    def core_copy(d, q):
        source = lax.rem(r + R - 2 * d, R)
        return pltpu.make_async_remote_copy(
            src_ref=rights.at[source, q],
            dst_ref=rights.at[source, q],
            send_sem=core_send.at[d, q],
            recv_sem=right_recv.at[source, q],
            device_id={"row": sibling},
        )

    def right_arrival(source, q):
        return pltpu.make_async_remote_copy(
            src_ref=rights.at[source, q],
            dst_ref=rights.at[source, q],
            send_sem=core_send.at[0, q],
            recv_sem=right_recv.at[source, q],
            device_id={"row": sibling},
        )

    def sum_copy(dest, p):
        return pltpu.make_async_remote_copy(
            src_ref=outbox.at[dest, p],
            dst_ref=inbox.at[c, p],
            send_sem=sum_send.at[dest, p],
            recv_sem=sum_recv.at[c, p],
            device_id={"col": dest},
        )

    def sum_arrival(source, p):
        return pltpu.make_async_remote_copy(
            src_ref=outbox.at[source, p],
            dst_ref=inbox.at[source, p],
            send_sem=sum_send.at[source, p],
            recv_sem=sum_recv.at[source, p],
            device_id={"col": source},
        )

    def gated(base, columns, target, rounded):
        tokens = pl.ds(pl.multiple_of(base * cols, G * cols), G * cols)
        product = jnp.dot(normed[tokens, :], w_in_ref[:, columns], preferred_element_type=F32)
        for i in range(G):
            block = product[i * cols : (i + 1) * cols]
            mask = row_live[pl.ds(base + i, 1), :] * col_live[...]
            value = jax.nn.sigmoid(block[:, :C]) * block[:, C:] * mask
            if rounded:
                value = value.astype(BF16).astype(F32)
            target[pl.ds(pl.multiple_of((base + i) * cols, cols), cols), :] = value

    def right_group(g, carry):
        base = g * G
        for i in range(G):
            same = row_chain[pl.ds(base + i, 1), :] == col_chain[...]
            pair_in = pair_ref[base + i] + jnp.where(same, chain_bias_ref[...], 0.0)
            tokens = pl.ds(pl.multiple_of((base + i) * cols, cols), cols)
            normed[tokens, :] = layer_norm(pair_in, gain_ref[...], bias_ref[...]).astype(BF16)
        gated(base, slice(2 * C, 4 * C), right, False)
        return carry

    for q in range(chunks):
        lax.fori_loop(q * (J // G), (q + 1) * (J // G), right_group, 0)
        for k in range(cols):
            rights[r, q, k] = right[pl.ds(q * J * cols + k, J, stride=cols), :].astype(BF16)
        if q == 0:
            pl.semaphore_wait(barrier, 1 + (half - 1) + (N - 1))
        for d in range(1, half):
            direct_copy(d, q).start()
        core_copy(0, q).start()

    def left_group(g, carry):
        gated(g * G, slice(0, 2 * C), left, True)
        return carry

    lax.fori_loop(0, rows // G, left_group, 0)

    def block(source, q):
        start = source * rows + q * J
        dest = start // cols
        p = lax.rem(start, cols) // J
        for k in range(cols):
            right_k[k] = rights[source, q, k].astype(F32)

        def group(g, carry):
            totals = [jnp.zeros((J, C), F32)] * G
            for k in range(cols):
                factor = right_k[k]
                for i in range(G):
                    totals[i] += left[pl.ds((g * G + i) * cols + k, 1), :] * factor

            @pl.when(dest == c)
            def _():
                for i in range(G):
                    own[p, g * G + i] = totals[i]

            @pl.when(dest != c)
            def _():
                for i in range(G):
                    outbox[dest, p, g * G + i] = totals[i].astype(BF16)

            return carry

        lax.fori_loop(0, rows // G, group, 0)

        @pl.when(dest != c)
        def _():
            sum_copy(dest, p).start()

    for d in range(half):
        source = lax.rem(r + R - 2 * d, R)
        other = lax.rem(sibling + R - 2 * d, R)

        def mine(q, carry):
            if d > 0:
                right_arrival(source, q).wait_recv()
                core_copy(d, q).start()
            block(source, q)
            return carry

        def siblings(q, carry):
            right_arrival(other, q).wait_recv()
            block(other, q)
            return carry

        lax.fori_loop(0, chunks, mine, 0)
        lax.fori_loop(0, chunks, siblings, 0)

    def gate_group(g, carry):
        tokens = pl.ds(pl.multiple_of(g * G * cols, G * cols), G * cols)
        product = jnp.dot(normed[tokens, :], w_in_ref[:, 4 * C :], preferred_element_type=F32)
        out_ref[pl.ds(g * G, G)] = jax.nn.sigmoid(product).reshape(G, cols, C)
        return carry

    lax.fori_loop(0, rows // G, gate_group, 0)

    for p in range(parts):
        for d in range(1, N):
            sum_arrival(lax.rem(c + d, N), p).wait_recv()

        def final_group(g, carry):
            group = pl.ds(g * G, G)
            mixed = own[p, group]
            for d in range(1, N):
                mixed += inbox[lax.rem(c + d, N), p, group].astype(F32)
            mixed_norm = layer_norm(mixed.reshape(G * J, C), out_gain_ref[...], out_bias_ref[...])
            update = jnp.dot(mixed_norm.astype(BF16), w_out_ref[...], preferred_element_type=F32)
            where = (group, pl.ds(p * J, J))
            out_ref[where] = out_ref[where] * update.reshape(G, J, C)
            return carry

        lax.fori_loop(0, rows // G, final_group, 0)

    for q in range(chunks):
        for d in range(half):
            if d > 0:
                direct_copy(d, q).wait_send()
            core_copy(d, q).wait_send()
    for d in range(1, N):
        for p in range(parts):
            sum_copy(lax.rem(c + d, N), p).wait_send()


def solution(mesh):
    R, N = mesh.shape["row"], mesh.shape["col"]

    def per_device(
        pair_rep,
        chain_ids,
        residue_mask,
        norm_gain,
        norm_bias,
        chain_bias,
        proj_in,
        out_gain,
        out_bias,
        proj_out,
    ):
        rows, cols, _ = pair_rep.shape
        chunks, parts = rows // J, cols // J
        tokens = rows * cols
        dma = pltpu.SemaphoreType.DMA
        update = pl.pallas_call(
            functools.partial(kernel, R, N),
            out_shape=jax.ShapeDtypeStruct(pair_rep.shape, F32),
            in_specs=[pl.BlockSpec(memory_space=pltpu.VMEM)] * 10,
            out_specs=pl.BlockSpec(memory_space=pltpu.VMEM),
            scratch_shapes=[
                pltpu.VMEM((rows, C), F32),
                pltpu.VMEM((cols, C), F32),
                pltpu.VMEM((rows, C), F32),
                pltpu.VMEM((cols, C), F32),
                pltpu.VMEM((tokens, C), BF16),
                pltpu.VMEM((tokens, C), F32),
                pltpu.VMEM((tokens, C), F32),
                pltpu.VMEM((cols, J, C), F32),
                pltpu.VMEM((R, chunks, cols, J, C), BF16),
                pltpu.VMEM((parts, rows, J, C), F32),
                pltpu.VMEM((N, parts, rows, J, C), BF16),
                pltpu.VMEM((N, parts, rows, J, C), BF16),
                dma((R // 2, chunks)),
                dma((R // 2, chunks)),
                dma((R, chunks)),
                dma((N, parts)),
                dma((N, parts)),
            ],
            compiler_params=pltpu.CompilerParams(
                collective_id=0, has_side_effects=True, vmem_limit_bytes=48 * 1024 * 1024
            ),
        )(
            pair_rep,
            chain_ids.reshape(1, -1),
            residue_mask.reshape(1, -1),
            norm_gain.reshape(1, C),
            norm_bias.reshape(1, C),
            chain_bias.reshape(1, C),
            proj_in,
            out_gain.reshape(1, C),
            out_bias.reshape(1, C),
            proj_out,
        )
        return pair_rep + update

    return jax.shard_map(
        per_device,
        mesh=mesh,
        in_specs=(
            P(("groups", "row"), "col", None),
            P("groups"),
            P("groups"),
            P(),
            P(),
            P(),
            P(),
            P(),
            P(),
            P(),
        ),
        out_specs=P(("groups", "row"), "col", None),
        check_vma=False,
    )
```

time: 132 us -> 37.4 us (0.28); the launches traced: 130 us -> 37.2 us
  waiting for transfers between devices: 92.2 us -> 0 us
  Pallas kernels: 0 us -> 32.8 us
  between operations: 13.2 us -> 0.05 us
  matrix products: 7.64 us -> 0 us
  other arithmetic: 7.53 us -> 0.88 us
  local copies, waits for them, and re-layouts: 9.07 us -> 3.42 us
    all_gather x2 -> x0, waiting for transfers between devices: 54.8 us -> none  [the longest x1 28 us: per_device(): lax.all_gather(left, 'col', axis=1, tiled=True)]
    psum x1 -> x0, waiting for transfers between devices: 36.7 us -> none  [broadcast(): return lax.psum(block, axis)]
    pallas_call x0 -> x1, Pallas kernels: none -> 32.8 us  [per_device(): pl.pallas_call(functools.partial(kernel, R, N), out_shape=jax.ShapeDtypeS...]
    dot_general x3 -> x0, matrix products: 7.64 us -> none  [the longest x1 3.55 us: per_device(): jnp.einsum('ikc,jkc->ijc', lax.all_gather(left, 'col', axis=1, tiled=True...]
    reduce_sum x3 -> x0, other arithmetic: 4.38 us -> none  [the longest x2 2.96 us: layer_norm(): variance = jnp.mean(center * center, axis=-1, keepdims=True)]
    dot_general x1 -> x0, local copies, waits for them, and re-layouts: 3.63 us -> none  [per_device(): jnp.einsum('ikc,jkc->ijc', lax.all_gather(left, 'col', axis=1, tiled=True...]
    unnamed x10 -> x20, local copies, waits for them, and re-layouts: 0.02 us -> 3.42 us
    all_gather x1 -> x0, local copies, waits for them, and re-layouts: 2.68 us -> none  [per_device(): lax.all_gather(left, 'col', axis=1, tiled=True)]
  transfers between devices with their start and end apart: 3 -> 0, of which waited for: 3 -> 0; matrix products, arithmetic and copies ran while one was open for 3% -> 0% of each run, Pallas kernels for 0% -> 0%
where the time goes in v1:
time: 37.4 us; the launch traced here: 37.2 us
  Pallas kernels  32.8 us (88%)
  local copies, waits for them, and re-layouts  3.42 us (9%)
  other arithmetic  0.88 us (2%)
    pallas_call x1, Pallas kernels, per_device(): pl.pallas_call(functools.partial(kernel, R, N), out_shape=jax.ShapeDtypeS...  32.8 us
    unnamed x20, local copies, waits for them, and re-layouts  3.42 us
    add x1, other arithmetic, per_device(): return pair_rep + update  0.88 us

profile of v1, /device:TPU:24, one launch (start us, length us, event | category | flops | bytes accessed | tf_op | source)
XLA Modules:
  0.0 37.2 jit_solution(9354096851643395561)
XLA Ops:
  0.0 0.0 copy-start.6
  0.0 0.0 copy-start.7
  0.0 0.0 copy-start.8
  0.0 0.0 copy-start.9
  0.0 0.0 copy-start.3
  0.0 0.0 copy-start.4
  0.0 0.0 copy-start.5
  0.0 0.6 %copy-done.6 = f32[128]{0:T(128)S(1)} copy-done((f32[128]{0:T(128)S(1)}, f32[128]{0:T(128)}, u32[]{:S(2)}) %copy-start.6) | copy-done | bytes 536
  0.7 0.0 copy-done.7
  0.7 0.0 copy-done.8
  0.7 0.0 copy-done.9
  0.7 0.0 copy-done.3
  0.7 0.0 copy-done.4
  0.7 0.0 copy-done.5
  0.8 0.0 copy-start
  0.8 1.0 %copy-done = f32[32,32,128]{2,1,0:T(8,128)S(1)} copy-done((f32[32,32,128]{2,1,0:T(8,128)S(1)}, f32[32,32,128]{2,1,0:T(8,128)}, u32[]{:S(2)}) %copy-start) | copy-done | bytes 524312
  1.8 0.0 copy-start.1
  1.8 0.9 %copy-done.1 = bf16[128,640]{1,0:T(8,128)(2,1)S(1)} copy-done((bf16[128,640]{1,0:T(8,128)(2,1)S(1)}, bf16[128,640]{1,0:T(8,128)(2,1)}, u32[]{:S(2)}) %copy-start.1) | copy-done | bytes 163864
  2.7 0.0 copy-start.2
  2.7 0.8 %copy-done.2 = bf16[128,128]{1,0:T(8,128)(2,1)S(1)} copy-done((bf16[128,128]{1,0:T(8,128)(2,1)S(1)}, bf16[128,128]{1,0:T(8,128)(2,1)}, u32[]{:S(2)}) %copy-start.2) | copy-done | bytes 32792
  3.5 32.8 %shard_map.100 = f32[32,32,128]{2,1,0:T(8,128)S(1)} custom-call(f32[32,32,128]{2,1,0:T(8,128)S(1)} %copy-done, s32[1,128]{1,0:T(1,128)S(1)} %bitcast.7, s32[1,128]{1,0:T(1,128)S(1)} %bitcast.8, f32[1,128]{1,0:T(1,128)S(1)} %bitcast.9, f32[1,128]{1,0:T(1,128)S(1)} %bitcast.10, f32[1,128]{1,0:T(1,128)S(1)} %bitcast.11, bf16[128,640]{1,0:T(8,128)(2,1)S(1)} %copy-done.1, ...), custom_call_target="tpu_custom_call" | custom-call | tf_op jit(solution)/shard_map/pallas_call | solution.py:272
  36.3 0.9 %add.3 = f32[32,32,128]{2,1,0:T(8,128)} add(f32[32,32,128]{2,1,0:T(8,128)S(1)} %copy-done, f32[32,32,128]{2,1,0:T(8,128)S(1)} %shard_map.100) | non-fusion elementwise | flops 131072 | bytes 1572864 | tf_op jit(solution)/shard_map/add | solution.py:311
Async XLA Ops:
  0.0 0.7 %copy-start.6 = (f32[128]{0:T(128)S(1)}, f32[128]{0:T(128)}, u32[]{:S(2)}) copy-start(f32[128]{0:T(128)} %param.14) | copy-start | bytes 1540
  0.0 0.7 %copy-start.7 = (f32[128]{0:T(128)S(1)}, f32[128]{0:T(128)}, u32[]{:S(2)}) copy-start(f32[128]{0:T(128)} %param.15) | copy-start | bytes 1540
  0.0 0.7 %copy-start.8 = (f32[128]{0:T(128)S(1)}, f32[128]{0:T(128)}, u32[]{:S(2)}) copy-start(f32[128]{0:T(128)} %param.17) | copy-start | bytes 1540
  0.0 0.7 %copy-start.9 = (f32[128]{0:T(128)S(1)}, f32[128]{0:T(128)}, u32[]{:S(2)}) copy-start(f32[128]{0:T(128)} %param.18) | copy-start | bytes 1540
  0.0 0.7 %copy-start.3 = (s32[128]{0:T(128)S(1)}, s32[128]{0:T(128)}, u32[]{:S(2)}) copy-start(s32[128]{0:T(128)} %param.11) | copy-start | bytes 1540
  0.0 0.7 %copy-start.4 = (s32[128]{0:T(128)S(1)}, s32[128]{0:T(128)}, u32[]{:S(2)}) copy-start(s32[128]{0:T(128)} %param.12) | copy-start | bytes 1540
  0.0 0.7 %copy-start.5 = (f32[128]{0:T(128)S(1)}, f32[128]{0:T(128)}, u32[]{:S(2)}) copy-start(f32[128]{0:T(128)} %param.13) | copy-start | bytes 1540
  0.8 1.0 %copy-start = (f32[32,32,128]{2,1,0:T(8,128)S(1)}, f32[32,32,128]{2,1,0:T(8,128)}, u32[]{:S(2)}) copy-start(f32[32,32,128]{2,1,0:T(8,128)} %pair_ref.1) | copy-start | bytes 1572868
  1.8 0.9 %copy-start.1 = (bf16[128,640]{1,0:T(8,128)(2,1)S(1)}, bf16[128,640]{1,0:T(8,128)(2,1)}, u32[]{:S(2)}) copy-start(bf16[128,640]{1,0:T(8,128)(2,1)} %w_in_ref.1) | copy-start | bytes 491524
  2.7 0.8 %copy-start.2 = (bf16[128,128]{1,0:T(8,128)(2,1)S(1)}, bf16[128,128]{1,0:T(8,128)(2,1)}, u32[]{:S(2)}) copy-start(bf16[128,128]{1,0:T(8,128)(2,1)} %w_out_ref.1) | copy-start | bytes 98308

commit v2 on v1

--- a/solution.py
+++ b/solution.py
@@ -1,4 +1,5 @@
 import functools
+import math
 
 import jax
 import jax.numpy as jnp
@@ -32,6 +33,17 @@
 def kernel(
     R,
     N,
+    pair_hbm,
+    chain_hbm,
+    mask_hbm,
+    gain_hbm,
+    bias_hbm,
+    chain_bias_hbm,
+    w_in_hbm,
+    out_gain_hbm,
+    out_bias_hbm,
+    w_out_hbm,
+    out_ref,
     pair_ref,
     chain_ref,
     mask_ref,
@@ -42,7 +54,6 @@
     out_gain_ref,
     out_bias_ref,
     w_out_ref,
-    out_ref,
     row_chain,
     col_chain,
     row_live,
@@ -52,14 +63,17 @@
     right,
     right_k,
     rights,
-    own,
+    kept,
     outbox,
     inbox,
+    load_sem,
+    pair_sem,
     direct_send,
     core_send,
     right_recv,
     sum_send,
     sum_recv,
+    pass_recv,
 ):
     rows, cols, _ = pair_ref.shape
     chunks = rows // J
@@ -69,6 +83,29 @@
     sibling = r + 1 - 2 * lax.rem(r, 2)
     half = R // 2
 
+    smalls = [
+        (chain_hbm, chain_ref),
+        (mask_hbm, mask_ref),
+        (gain_hbm, gain_ref),
+        (bias_hbm, bias_ref),
+        (chain_bias_hbm, chain_bias_ref),
+        (w_in_hbm, w_in_ref),
+        (out_gain_hbm, out_gain_ref),
+        (out_bias_hbm, out_bias_ref),
+        (w_out_hbm, w_out_ref),
+    ]
+    loads = [
+        pltpu.make_async_copy(src, dst, load_sem.at[n]) for n, (src, dst) in enumerate(smalls)
+    ]
+    pair_loads = [
+        pltpu.make_async_copy(
+            pair_hbm.at[pl.ds(q * J, J)], pair_ref.at[pl.ds(q * J, J)], pair_sem.at[q]
+        )
+        for q in range(chunks)
+    ]
+    for load in loads[:2] + pair_loads[:1] + loads[2:] + pair_loads[1:]:
+        load.start()
+
     barrier = pltpu.get_barrier_semaphore()
     pl.semaphore_signal(barrier, inc=1, device_id={"row": sibling})
     for d in range(1, half):
@@ -76,6 +113,8 @@
     for d in range(1, N):
         pl.semaphore_signal(barrier, inc=1, device_id={"col": lax.rem(c + d, N)})
 
+    for load in loads[:2]:
+        load.wait()
     row_chain[...] = as_rows(chain_ref, r * rows, rows)
     col_chain[...] = as_rows(chain_ref, c * cols, cols)
     row_live[...] = as_rows(mask_ref, r * rows, rows)
@@ -107,6 +146,39 @@
             send_sem=core_send.at[0, q],
             recv_sem=right_recv.at[source, q],
             device_id={"row": sibling},
+        )
+
+    def passes_on(device, dest):
+        if N < 4:
+            return False
+        low = jnp.logical_and(device == 0, dest >= 2)
+        return jnp.logical_or(low, jnp.logical_and(device == N - 1, dest <= N - 3))
+
+    def adds_to(device, dest):
+        if N < 4:
+            return False
+        low = jnp.logical_and(device == 1, dest >= 2)
+        return jnp.logical_or(low, jnp.logical_and(device == N - 2, dest <= N - 3))
+
+    inner = jnp.where(c == 0, 1, N - 2)
+    outer = jnp.where(c == 1, 0, N - 1)
+
+    def pass_copy(dest, p):
+        return pltpu.make_async_remote_copy(
+            src_ref=outbox.at[dest, p],
+            dst_ref=outbox.at[dest, p],
+            send_sem=sum_send.at[dest, p],
+            recv_sem=pass_recv.at[dest, p],
+            device_id={"col": inner},
+        )
+
+    def pass_arrival(dest, p):
+        return pltpu.make_async_remote_copy(
+            src_ref=outbox.at[dest, p],
+            dst_ref=outbox.at[dest, p],
+            send_sem=sum_send.at[dest, p],
+            recv_sem=pass_recv.at[dest, p],
+            device_id={"col": outer},
         )
 
     def sum_copy(dest, p):
@@ -138,18 +210,21 @@
                 value = value.astype(BF16).astype(F32)
             target[pl.ds(pl.multiple_of((base + i) * cols, cols), cols), :] = value
 
-    def right_group(g, carry):
-        base = g * G
-        for i in range(G):
+    def right_group(base):
+        for i in range(J):
             same = row_chain[pl.ds(base + i, 1), :] == col_chain[...]
             pair_in = pair_ref[base + i] + jnp.where(same, chain_bias_ref[...], 0.0)
             tokens = pl.ds(pl.multiple_of((base + i) * cols, cols), cols)
             normed[tokens, :] = layer_norm(pair_in, gain_ref[...], bias_ref[...]).astype(BF16)
-        gated(base, slice(2 * C, 4 * C), right, False)
-        return carry
+        for g in range(J // G):
+            gated(base + g * G, slice(2 * C, 4 * C), right, False)
 
     for q in range(chunks):
-        lax.fori_loop(q * (J // G), (q + 1) * (J // G), right_group, 0)
+        if q == 0:
+            for load in loads[2:6]:
+                load.wait()
+        pair_loads[q].wait()
+        right_group(q * J)
         for k in range(cols):
             rights[r, q, k] = right[pl.ds(q * J * cols + k, J, stride=cols), :].astype(BF16)
         if q == 0:
@@ -158,16 +233,20 @@
             direct_copy(d, q).start()
         core_copy(0, q).start()
 
-    def left_group(g, carry):
-        gated(g * G, slice(0, 2 * C), left, True)
+    def left_group(q, carry):
+        for g in range(J // G):
+            gated(q * J + g * G, slice(0, 2 * C), left, True)
         return carry
 
-    lax.fori_loop(0, rows // G, left_group, 0)
+    lax.fori_loop(0, chunks, left_group, 0)
+
+    def dest_of(source, q):
+        start = source * rows + q * J
+        return start // cols, lax.rem(start, cols) // J
 
     def block(source, q):
-        start = source * rows + q * J
-        dest = start // cols
-        p = lax.rem(start, cols) // J
+        dest, p = dest_of(source, q)
+        keep = jnp.logical_or(dest == c, adds_to(c, dest))
         for k in range(cols):
             right_k[k] = rights[source, q, k].astype(F32)
 
@@ -178,12 +257,12 @@
                 for i in range(G):
                     totals[i] += left[pl.ds((g * G + i) * cols + k, 1), :] * factor
 
-            @pl.when(dest == c)
+            @pl.when(keep)
             def _():
                 for i in range(G):
-                    own[p, g * G + i] = totals[i]
-
-            @pl.when(dest != c)
+                    kept[dest, p, g * G + i] = totals[i]
+
+            @pl.when(jnp.logical_not(keep))
             def _():
                 for i in range(G):
                     outbox[dest, p, g * G + i] = totals[i].astype(BF16)
@@ -192,8 +271,33 @@
 
         lax.fori_loop(0, rows // G, group, 0)
 
-        @pl.when(dest != c)
+        @pl.when(jnp.logical_not(keep))
         def _():
+            if N < 4:
+                sum_copy(dest, p).start()
+            else:
+
+                @pl.when(passes_on(c, dest))
+                def _():
+                    pass_copy(dest, p).start()
+
+                @pl.when(jnp.logical_not(passes_on(c, dest)))
+                def _():
+                    sum_copy(dest, p).start()
+
+    def forward(source, q):
+        dest, p = dest_of(source, q)
+
+        @pl.when(adds_to(c, dest))
+        def _():
+            pass_arrival(dest, p).wait_recv()
+
+            def group(g, carry):
+                where = (dest, p, pl.ds(g * G, G))
+                outbox[where] = (kept[where] + outbox[where].astype(F32)).astype(BF16)
+                return carry
+
+            lax.fori_loop(0, rows // G, group, 0)
             sum_copy(dest, p).start()
 
     for d in range(half):
@@ -215,6 +319,16 @@
         lax.fori_loop(0, chunks, mine, 0)
         lax.fori_loop(0, chunks, siblings, 0)
 
+    if N >= 4:
+        for d in range(half):
+            for source in (lax.rem(r + R - 2 * d, R), lax.rem(sibling + R - 2 * d, R)):
+
+                def passed(q, carry):
+                    forward(source, q)
+                    return carry
+
+                lax.fori_loop(0, chunks, passed, 0)
+
     def gate_group(g, carry):
         tokens = pl.ds(pl.multiple_of(g * G * cols, G * cols), G * cols)
         product = jnp.dot(normed[tokens, :], w_in_ref[:, 4 * C :], preferred_element_type=F32)
@@ -223,22 +337,45 @@
 
     lax.fori_loop(0, rows // G, gate_group, 0)
 
+    for load in loads[6:]:
+        load.wait()
+
+    if N < 4:
+        sources = [lax.rem(c + d, N) for d in range(1, N)]
+    else:
+        ends = jnp.where(c == 1, 0, jnp.where(c == N - 2, N - 1, c))
+        sources = [jnp.where(c == n, ends, n) for n in range(1, N - 1)]
+
     for p in range(parts):
-        for d in range(1, N):
-            sum_arrival(lax.rem(c + d, N), p).wait_recv()
+        for source in sources:
+            if N <= 4:
+                sum_arrival(source, p).wait_recv()
+            else:
+
+                @pl.when(source != c)
+                def _():
+                    sum_arrival(source, p).wait_recv()
+
+                    def collect(g, carry):
+                        group = pl.ds(g * G, G)
+                        kept[c, p, group] += inbox[source, p, group].astype(F32)
+                        return carry
+
+                    lax.fori_loop(0, rows // G, collect, 0)
 
         def final_group(g, carry):
-            group = pl.ds(g * G, G)
-            mixed = own[p, group]
-            for d in range(1, N):
-                mixed += inbox[lax.rem(c + d, N), p, group].astype(F32)
-            mixed_norm = layer_norm(mixed.reshape(G * J, C), out_gain_ref[...], out_bias_ref[...])
+            group = pl.ds(g * J, J)
+            mixed = kept[c, p, group]
+            if N <= 4:
+                for source in sources:
+                    mixed += inbox[source, p, group].astype(F32)
+            mixed_norm = layer_norm(mixed.reshape(J * J, C), out_gain_ref[...], out_bias_ref[...])
             update = jnp.dot(mixed_norm.astype(BF16), w_out_ref[...], preferred_element_type=F32)
             where = (group, pl.ds(p * J, J))
-            out_ref[where] = out_ref[where] * update.reshape(G, J, C)
+            out_ref[where] = out_ref[where] * update.reshape(J, J, C)
             return carry
 
-        lax.fori_loop(0, rows // G, final_group, 0)
+        lax.fori_loop(0, chunks, final_group, 0)
 
     for q in range(chunks):
         for d in range(half):
@@ -269,32 +406,49 @@
         chunks, parts = rows // J, cols // J
         tokens = rows * cols
         dma = pltpu.SemaphoreType.DMA
+        buffers = [
+            pltpu.VMEM(pair_rep.shape, F32),
+            pltpu.VMEM((1, chain_ids.shape[0]), jnp.int32),
+            pltpu.VMEM((1, chain_ids.shape[0]), jnp.int32),
+            pltpu.VMEM((1, C), F32),
+            pltpu.VMEM((1, C), F32),
+            pltpu.VMEM((1, C), F32),
+            pltpu.VMEM(proj_in.shape, BF16),
+            pltpu.VMEM((1, C), F32),
+            pltpu.VMEM((1, C), F32),
+            pltpu.VMEM(proj_out.shape, BF16),
+            pltpu.VMEM((rows, C), F32),
+            pltpu.VMEM((cols, C), F32),
+            pltpu.VMEM((rows, C), F32),
+            pltpu.VMEM((cols, C), F32),
+            pltpu.VMEM((tokens, C), BF16),
+            pltpu.VMEM((tokens, C), F32),
+            pltpu.VMEM((tokens, C), F32),
+            pltpu.VMEM((cols, J, C), F32),
+            pltpu.VMEM((R, chunks, cols, J, C), BF16),
+            pltpu.VMEM((N, parts, rows, J, C), F32),
+            pltpu.VMEM((N, parts, rows, J, C), BF16),
+            pltpu.VMEM((N, parts, rows, J, C), BF16),
+        ]
+        semaphores = [
+            dma((9,)),
+            dma((chunks,)),
+            dma((R // 2, chunks)),
+            dma((R // 2, chunks)),
+            dma((R, chunks)),
+            dma((N, parts)),
+            dma((N, parts)),
+            dma((N, parts)),
+        ]
+        held = sum(math.prod(b.shape) * jnp.dtype(b.dtype).itemsize for b in buffers)
         update = pl.pallas_call(
             functools.partial(kernel, R, N),
             out_shape=jax.ShapeDtypeStruct(pair_rep.shape, F32),
-            in_specs=[pl.BlockSpec(memory_space=pltpu.VMEM)] * 10,
+            in_specs=[pl.BlockSpec(memory_space=pltpu.HBM)] * 10,
             out_specs=pl.BlockSpec(memory_space=pltpu.VMEM),
-            scratch_shapes=[
-                pltpu.VMEM((rows, C), F32),
-                pltpu.VMEM((cols, C), F32),
-                pltpu.VMEM((rows, C), F32),
-                pltpu.VMEM((cols, C), F32),
-                pltpu.VMEM((tokens, C), BF16),
-                pltpu.VMEM((tokens, C), F32),
-                pltpu.VMEM((tokens, C), F32),
-                pltpu.VMEM((cols, J, C), F32),
-                pltpu.VMEM((R, chunks, cols, J, C), BF16),
-                pltpu.VMEM((parts, rows, J, C), F32),
-                pltpu.VMEM((N, parts, rows, J, C), BF16),
-                pltpu.VMEM((N, parts, rows, J, C), BF16),
-                dma((R // 2, chunks)),
-                dma((R // 2, chunks)),
-                dma((R, chunks)),
-                dma((N, parts)),
-                dma((N, parts)),
-            ],
+            scratch_shapes=buffers + semaphores,
             compiler_params=pltpu.CompilerParams(
-                collective_id=0, has_side_effects=True, vmem_limit_bytes=48 * 1024 * 1024
+                collective_id=0, has_side_effects=True, vmem_limit_bytes=held + 8 * 1024 * 1024
             ),
         )(
             pair_rep,

time: 37.4 us -> 34.9 us (0.933)
  the two profiles are of different devices: /device:TPU:24 before, /device:TPU:3 now
where the time goes in v2:
time: 34.9 us; the launch traced here: 34.7 us
  Pallas kernels  30.3 us (87%)
  local copies, waits for them, and re-layouts  3.42 us (10%)
  other arithmetic  0.88 us (3%)
    pallas_call x1, Pallas kernels, per_device(): pl.pallas_call(functools.partial(kernel, R, N), out_shape=jax.ShapeDtypeS...  30.3 us
    unnamed x20, local copies, waits for them, and re-layouts  3.42 us
    add x1, other arithmetic, per_device(): return pair_rep + update  0.88 us

profile of v2, /device:TPU:3, one launch (start us, length us, event | category | flops | bytes accessed | tf_op | source)
XLA Modules:
  0.0 34.7 jit_solution(11325393516550608396)
XLA Ops:
  0.0 0.0 copy-start.6
  0.0 0.0 copy-start.7
  0.0 0.0 copy-start.8
  0.0 0.0 copy-start.9
  0.0 0.0 copy-start.3
  0.0 0.0 copy-start.4
  0.0 0.0 copy-start.5
  0.0 0.6 %copy-done.6 = f32[128]{0:T(128)S(1)} copy-done((f32[128]{0:T(128)S(1)}, f32[128]{0:T(128)}, u32[]{:S(2)}) %copy-start.6) | copy-done | bytes 536
  0.7 0.0 copy-done.7
  0.7 0.0 copy-done.8
  0.7 0.0 copy-done.9
  0.7 0.0 copy-done.3
  0.7 0.0 copy-done.4
  0.7 0.0 copy-done.5
  0.8 0.0 copy-start
  0.8 1.0 %copy-done = f32[32,32,128]{2,1,0:T(8,128)S(1)} copy-done((f32[32,32,128]{2,1,0:T(8,128)S(1)}, f32[32,32,128]{2,1,0:T(8,128)}, u32[]{:S(2)}) %copy-start) | copy-done | bytes 524312
  1.8 0.0 copy-start.1
  1.8 0.9 %copy-done.1 = bf16[128,640]{1,0:T(8,128)(2,1)S(1)} copy-done((bf16[128,640]{1,0:T(8,128)(2,1)S(1)}, bf16[128,640]{1,0:T(8,128)(2,1)}, u32[]{:S(2)}) %copy-start.1) | copy-done | bytes 163864
  2.7 0.0 copy-start.2
  2.7 0.8 %copy-done.2 = bf16[128,128]{1,0:T(8,128)(2,1)S(1)} copy-done((bf16[128,128]{1,0:T(8,128)(2,1)S(1)}, bf16[128,128]{1,0:T(8,128)(2,1)}, u32[]{:S(2)}) %copy-start.2) | copy-done | bytes 32792
  3.5 30.3 %shard_map.100 = f32[32,32,128]{2,1,0:T(8,128)S(1)} custom-call(f32[32,32,128]{2,1,0:T(8,128)S(1)} %copy-done, s32[1,128]{1,0:T(1,128)S(1)} %bitcast.7, s32[1,128]{1,0:T(1,128)S(1)} %bitcast.8, f32[1,128]{1,0:T(1,128)S(1)} %bitcast.9, f32[1,128]{1,0:T(1,128)S(1)} %bitcast.10, f32[1,128]{1,0:T(1,128)S(1)} %bitcast.11, bf16[128,640]{1,0:T(8,128)(2,1)S(1)} %copy-done.1, ...), custom_call_target="tpu_custom_call" | custom-call | tf_op jit(solution)/shard_map/pallas_call | solution.py:444
  33.8 0.9 %add.3 = f32[32,32,128]{2,1,0:T(8,128)} add(f32[32,32,128]{2,1,0:T(8,128)S(1)} %copy-done, f32[32,32,128]{2,1,0:T(8,128)S(1)} %shard_map.100) | non-fusion elementwise | flops 131072 | bytes 1572864 | tf_op jit(solution)/shard_map/add | solution.py:465
Async XLA Ops:
  0.0 0.7 %copy-start.6 = (f32[128]{0:T(128)S(1)}, f32[128]{0:T(128)}, u32[]{:S(2)}) copy-start(f32[128]{0:T(128)} %param.14) | copy-start | bytes 1540
  0.0 0.7 %copy-start.7 = (f32[128]{0:T(128)S(1)}, f32[128]{0:T(128)}, u32[]{:S(2)}) copy-start(f32[128]{0:T(128)} %param.15) | copy-start | bytes 1540
  0.0 0.7 %copy-start.8 = (f32[128]{0:T(128)S(1)}, f32[128]{0:T(128)}, u32[]{:S(2)}) copy-start(f32[128]{0:T(128)} %param.17) | copy-start | bytes 1540
  0.0 0.7 %copy-start.9 = (f32[128]{0:T(128)S(1)}, f32[128]{0:T(128)}, u32[]{:S(2)}) copy-start(f32[128]{0:T(128)} %param.18) | copy-start | bytes 1540
  0.0 0.7 %copy-start.3 = (s32[128]{0:T(128)S(1)}, s32[128]{0:T(128)}, u32[]{:S(2)}) copy-start(s32[128]{0:T(128)} %param.11) | copy-start | bytes 1540
  0.0 0.7 %copy-start.4 = (s32[128]{0:T(128)S(1)}, s32[128]{0:T(128)}, u32[]{:S(2)}) copy-start(s32[128]{0:T(128)} %param.12) | copy-start | bytes 1540
  0.0 0.7 %copy-start.5 = (f32[128]{0:T(128)S(1)}, f32[128]{0:T(128)}, u32[]{:S(2)}) copy-start(f32[128]{0:T(128)} %param.13) | copy-start | bytes 1540
  0.8 1.0 %copy-start = (f32[32,32,128]{2,1,0:T(8,128)S(1)}, f32[32,32,128]{2,1,0:T(8,128)}, u32[]{:S(2)}) copy-start(f32[32,32,128]{2,1,0:T(8,128)} %pair_hbm.1) | copy-start | bytes 1572868
  1.8 0.9 %copy-start.1 = (bf16[128,640]{1,0:T(8,128)(2,1)S(1)}, bf16[128,640]{1,0:T(8,128)(2,1)}, u32[]{:S(2)}) copy-start(bf16[128,640]{1,0:T(8,128)(2,1)} %w_in_hbm.1) | copy-start | bytes 491524
  2.7 0.8 %copy-start.2 = (bf16[128,128]{1,0:T(8,128)(2,1)S(1)}, bf16[128,128]{1,0:T(8,128)(2,1)}, u32[]{:S(2)}) copy-start(bf16[128,128]{1,0:T(8,128)(2,1)} %w_out_hbm.1) | copy-start | bytes 98308

commit v3 on v2

--- a/solution.py
+++ b/solution.py
@@ -11,6 +11,7 @@
 C = 128
 G = 8
 J = 16
+DEPTH = 2
 F32 = jnp.float32
 BF16 = jnp.bfloat16
 
@@ -74,6 +75,7 @@
     sum_send,
     sum_recv,
     pass_recv,
+    end_send,
 ):
     rows, cols, _ = pair_ref.shape
     chunks = rows // J
@@ -163,11 +165,11 @@
     inner = jnp.where(c == 0, 1, N - 2)
     outer = jnp.where(c == 1, 0, N - 1)
 
-    def pass_copy(dest, p):
+    def pass_copy(dest, p, send_sem):
         return pltpu.make_async_remote_copy(
             src_ref=outbox.at[dest, p],
             dst_ref=outbox.at[dest, p],
-            send_sem=sum_send.at[dest, p],
+            send_sem=send_sem,
             recv_sem=pass_recv.at[dest, p],
             device_id={"col": inner},
         )
@@ -181,11 +183,11 @@
             device_id={"col": outer},
         )
 
-    def sum_copy(dest, p):
+    def sum_copy(dest, p, send_sem=None):
         return pltpu.make_async_remote_copy(
             src_ref=outbox.at[dest, p],
             dst_ref=inbox.at[c, p],
-            send_sem=sum_send.at[dest, p],
+            send_sem=sum_send.at[dest, p] if send_sem is None else send_sem,
             recv_sem=sum_recv.at[c, p],
             device_id={"col": dest},
         )
@@ -244,7 +246,18 @@
         start = source * rows + q * J
         return start // cols, lax.rem(start, cols) // J
 
-    def block(source, q):
+    at_end = jnp.logical_or(c == 0, c == N - 1)
+
+    def send_slot(sent):
+        slot = end_send.at[lax.rem(sent, DEPTH)]
+
+        @pl.when(sent >= DEPTH)
+        def _():
+            sum_copy(inner, 0, slot).wait_send()
+
+        return slot
+
+    def block(source, q, sent):
         dest, p = dest_of(source, q)
         keep = jnp.logical_or(dest == c, adds_to(c, dest))
         for k in range(cols):
@@ -277,13 +290,24 @@
                 sum_copy(dest, p).start()
             else:
 
-                @pl.when(passes_on(c, dest))
-                def _():
-                    pass_copy(dest, p).start()
-
-                @pl.when(jnp.logical_not(passes_on(c, dest)))
+                @pl.when(jnp.logical_not(at_end))
                 def _():
                     sum_copy(dest, p).start()
+
+        if N < 4:
+            return sent
+        far = jnp.logical_and(at_end, passes_on(c, dest))
+        near = jnp.logical_and(at_end, jnp.logical_and(dest == inner, p == 0))
+
+        @pl.when(far)
+        def _():
+            pass_copy(dest, p, send_slot(sent)).start()
+
+        @pl.when(near)
+        def _():
+            sum_copy(dest, p, send_slot(sent)).start()
+
+        return sent + jnp.where(jnp.logical_or(far, near), 1, 0)
 
     def forward(source, q):
         dest, p = dest_of(source, q)
@@ -300,6 +324,7 @@
             lax.fori_loop(0, rows // G, group, 0)
             sum_copy(dest, p).start()
 
+    sent = jnp.int32(0)
     for d in range(half):
         source = lax.rem(r + R - 2 * d, R)
         other = lax.rem(sibling + R - 2 * d, R)
@@ -308,16 +333,21 @@
             if d > 0:
                 right_arrival(source, q).wait_recv()
                 core_copy(d, q).start()
-            block(source, q)
-            return carry
+            return block(source, q, carry)
 
         def siblings(q, carry):
             right_arrival(other, q).wait_recv()
-            block(other, q)
-            return carry
-
-        lax.fori_loop(0, chunks, mine, 0)
-        lax.fori_loop(0, chunks, siblings, 0)
+            return block(other, q, carry)
+
+        sent = lax.fori_loop(0, chunks, mine, sent)
+        sent = lax.fori_loop(0, chunks, siblings, sent)
+
+    if N >= 4:
+
+        @pl.when(at_end)
+        def _():
+            for p in range(1, parts):
+                sum_copy(inner, p, send_slot(sent + p - 1)).start()
 
     if N >= 4:
         for d in range(half):
@@ -382,9 +412,23 @@
             if d > 0:
                 direct_copy(d, q).wait_send()
             core_copy(d, q).wait_send()
-    for d in range(1, N):
-        for p in range(parts):
-            sum_copy(lax.rem(c + d, N), p).wait_send()
+    if N < 4:
+        for d in range(1, N):
+            for p in range(parts):
+                sum_copy(lax.rem(c + d, N), p).wait_send()
+    else:
+
+        @pl.when(jnp.logical_not(at_end))
+        def _():
+            for d in range(1, N):
+                for p in range(parts):
+                    sum_copy(lax.rem(c + d, N), p).wait_send()
+
+        @pl.when(at_end)
+        def _():
+            for n in range(DEPTH):
+                slot = end_send.at[lax.rem(sent + parts - 1 + n, DEPTH)]
+                sum_copy(inner, 0, slot).wait_send()
 
 
 def solution(mesh):
@@ -439,6 +483,7 @@
             dma((N, parts)),
             dma((N, parts)),
             dma((N, parts)),
+            dma((DEPTH,)),
         ]
         held = sum(math.prod(b.shape) * jnp.dtype(b.dtype).itemsize for b in buffers)
         update = pl.pallas_call(
@@ -448,7 +493,7 @@
             out_specs=pl.BlockSpec(memory_space=pltpu.VMEM),
             scratch_shapes=buffers + semaphores,
             compiler_params=pltpu.CompilerParams(
-                collective_id=0, has_side_effects=True, vmem_limit_bytes=held + 8 * 1024 * 1024
+                collective_id=0, has_side_effects=True, vmem_limit_bytes=max(held, 48 * 1024 * 1024) + 8 * 1024 * 1024
             ),
         )(
             pair_rep,

time: 34.9 us -> 30.6 us (0.88)
  the two profiles are of different devices: /device:TPU:3 before, /device:TPU:24 now
where the time goes in v3:
time: 30.6 us; the launch traced here: 30.5 us
  Pallas kernels  28.5 us (93%)
  other arithmetic  1.91 us (6%)
    pallas_call x1, Pallas kernels, per_device(): pl.pallas_call(functools.partial(kernel, R, N), out_shape=jax.ShapeDtypeS...  28.5 us
    add x1, other arithmetic, per_device(): return pair_rep + update  1.91 us

profile of v3, /device:TPU:24, one launch (start us, length us, event | category | flops | bytes accessed | tf_op | source)
XLA Modules:
  0.0 30.5 jit_solution(4133496778728978856)
XLA Ops:
  0.0 0.0 copy-start
  0.0 28.5 %shard_map.100 = f32[32,32,128]{2,1,0:T(8,128)} custom-call(f32[32,32,128]{2,1,0:T(8,128)} %pair_hbm.1, s32[1,128]{1,0:T(1,128)} %bitcast.7, s32[1,128]{1,0:T(1,128)} %bitcast.8, f32[1,128]{1,0:T(1,128)} %bitcast.9, f32[1,128]{1,0:T(1,128)} %bitcast.10, f32[1,128]{1,0:T(1,128)} %bitcast.11, bf16[128,640]{1,0:T(8,128)(2,1)} %w_in_hbm.1, f32[1,128]{1,0:T(1,128)} %bitcast.12, ...), custom_call_target="tpu_custom_call" | custom-call | tf_op jit(solution)/shard_map/pallas_call | solution.py:489
  28.5 0.0 copy-done
  28.5 1.9 %add.3 = f32[32,32,128]{2,1,0:T(8,128)} add(f32[32,32,128]{2,1,0:T(8,128)S(1)} %copy-done, f32[32,32,128]{2,1,0:T(8,128)} %shard_map.100) | non-fusion elementwise | flops 131072 | bytes 1572864 | tf_op jit(solution)/shard_map/add | solution.py:510
Async XLA Ops:
  0.0 28.5 %copy-start = (f32[32,32,128]{2,1,0:T(8,128)S(1)}, f32[32,32,128]{2,1,0:T(8,128)}, u32[]{:S(2)}) copy-start(f32[32,32,128]{2,1,0:T(8,128)} %pair_hbm.1) | copy-start | bytes 1572868

commit v4 on v3

--- a/solution.py
+++ b/solution.py
@@ -11,7 +11,8 @@
 C = 128
 G = 8
 J = 16
-DEPTH = 2
+H = 2
+DEPTH = 3
 F32 = jnp.float32
 BF16 = jnp.bfloat16
 
@@ -80,6 +81,8 @@
     rows, cols, _ = pair_ref.shape
     chunks = rows // J
     parts = cols // J
+    pieces = parts * H
+    tall = rows // H
     r = lax.axis_index("row")
     c = lax.axis_index("col")
     sibling = r + 1 - 2 * lax.rem(r, 2)
@@ -263,66 +266,68 @@
         for k in range(cols):
             right_k[k] = rights[source, q, k].astype(F32)
 
-        def group(g, carry):
-            totals = [jnp.zeros((J, C), F32)] * G
-            for k in range(cols):
-                factor = right_k[k]
-                for i in range(G):
-                    totals[i] += left[pl.ds((g * G + i) * cols + k, 1), :] * factor
-
-            @pl.when(keep)
-            def _():
-                for i in range(G):
-                    kept[dest, p, g * G + i] = totals[i]
+        for h in range(H):
+            piece = p * H + h
+
+            def group(g, carry):
+                totals = [jnp.zeros((J, C), F32)] * G
+                for k in range(cols):
+                    factor = right_k[k]
+                    for i in range(G):
+                        row = h * tall + g * G + i
+                        totals[i] += left[pl.ds(row * cols + k, 1), :] * factor
+
+                @pl.when(keep)
+                def _():
+                    for i in range(G):
+                        kept[dest, piece, g * G + i] = totals[i]
+
+                @pl.when(jnp.logical_not(keep))
+                def _():
+                    for i in range(G):
+                        outbox[dest, piece, g * G + i] = totals[i].astype(BF16)
+
+                return carry
+
+            lax.fori_loop(0, tall // G, group, 0)
 
             @pl.when(jnp.logical_not(keep))
             def _():
-                for i in range(G):
-                    outbox[dest, p, g * G + i] = totals[i].astype(BF16)
-
-            return carry
-
-        lax.fori_loop(0, rows // G, group, 0)
-
-        @pl.when(jnp.logical_not(keep))
-        def _():
-            if N < 4:
-                sum_copy(dest, p).start()
-            else:
-
-                @pl.when(jnp.logical_not(at_end))
+                if N < 4:
+                    sum_copy(dest, piece).start()
+                else:
+
+                    @pl.when(jnp.logical_not(at_end))
+                    def _():
+                        sum_copy(dest, piece).start()
+
+            if N >= 4:
+                far = jnp.logical_and(at_end, passes_on(c, dest))
+                near = jnp.logical_and(at_end, jnp.logical_and(dest == inner, p == 0))
+
+                @pl.when(far)
                 def _():
-                    sum_copy(dest, p).start()
-
-        if N < 4:
-            return sent
-        far = jnp.logical_and(at_end, passes_on(c, dest))
-        near = jnp.logical_and(at_end, jnp.logical_and(dest == inner, p == 0))
-
-        @pl.when(far)
-        def _():
-            pass_copy(dest, p, send_slot(sent)).start()
-
-        @pl.when(near)
-        def _():
-            sum_copy(dest, p, send_slot(sent)).start()
-
-        return sent + jnp.where(jnp.logical_or(far, near), 1, 0)
+                    pass_copy(dest, piece, send_slot(sent)).start()
+
+                @pl.when(near)
+                def _():
+                    sum_copy(dest, piece, send_slot(sent)).start()
+
+                sent = sent + jnp.where(jnp.logical_or(far, near), 1, 0)
+        return sent
 
     def forward(source, q):
         dest, p = dest_of(source, q)
 
         @pl.when(adds_to(c, dest))
         def _():
-            pass_arrival(dest, p).wait_recv()
-
-            def group(g, carry):
-                where = (dest, p, pl.ds(g * G, G))
-                outbox[where] = (kept[where] + outbox[where].astype(F32)).astype(BF16)
-                return carry
-
-            lax.fori_loop(0, rows // G, group, 0)
-            sum_copy(dest, p).start()
+            for h in range(H):
+                piece = p * H + h
+                pass_arrival(dest, piece).wait_recv()
+                for g in range(tall // G):
+                    where = (dest, piece, pl.ds(g * G, G))
+                    outbox[where] = (kept[where] + outbox[where].astype(F32)).astype(BF16)
+                sum_copy(dest, piece).start()
 
     sent = jnp.int32(0)
     for d in range(half):
@@ -346,8 +351,8 @@
 
         @pl.when(at_end)
         def _():
-            for p in range(1, parts):
-                sum_copy(inner, p, send_slot(sent + p - 1)).start()
+            for n in range(H, pieces):
+                sum_copy(inner, n, send_slot(sent + n - H)).start()
 
     if N >= 4:
         for d in range(half):
@@ -376,36 +381,37 @@
         ends = jnp.where(c == 1, 0, jnp.where(c == N - 2, N - 1, c))
         sources = [jnp.where(c == n, ends, n) for n in range(1, N - 1)]
 
-    for p in range(parts):
+    for piece in range(pieces):
+        p, h = piece // H, piece % H
         for source in sources:
             if N <= 4:
-                sum_arrival(source, p).wait_recv()
+                sum_arrival(source, piece).wait_recv()
             else:
 
                 @pl.when(source != c)
                 def _():
-                    sum_arrival(source, p).wait_recv()
+                    sum_arrival(source, piece).wait_recv()
 
                     def collect(g, carry):
                         group = pl.ds(g * G, G)
-                        kept[c, p, group] += inbox[source, p, group].astype(F32)
+                        kept[c, piece, group] += inbox[source, piece, group].astype(F32)
                         return carry
 
-                    lax.fori_loop(0, rows // G, collect, 0)
+                    lax.fori_loop(0, tall // G, collect, 0)
 
         def final_group(g, carry):
             group = pl.ds(g * J, J)
-            mixed = kept[c, p, group]
+            mixed = kept[c, piece, group]
             if N <= 4:
                 for source in sources:
-                    mixed += inbox[source, p, group].astype(F32)
+                    mixed += inbox[source, piece, group].astype(F32)
             mixed_norm = layer_norm(mixed.reshape(J * J, C), out_gain_ref[...], out_bias_ref[...])
             update = jnp.dot(mixed_norm.astype(BF16), w_out_ref[...], preferred_element_type=F32)
-            where = (group, pl.ds(p * J, J))
+            where = (pl.ds(h * tall + g * J, J), pl.ds(p * J, J))
             out_ref[where] = out_ref[where] * update.reshape(J, J, C)
             return carry
 
-        lax.fori_loop(0, chunks, final_group, 0)
+        lax.fori_loop(0, tall // J, final_group, 0)
 
     for q in range(chunks):
         for d in range(half):
@@ -414,20 +420,20 @@
             core_copy(d, q).wait_send()
     if N < 4:
         for d in range(1, N):
-            for p in range(parts):
-                sum_copy(lax.rem(c + d, N), p).wait_send()
+            for piece in range(pieces):
+                sum_copy(lax.rem(c + d, N), piece).wait_send()
     else:
 
         @pl.when(jnp.logical_not(at_end))
         def _():
             for d in range(1, N):
-                for p in range(parts):
-                    sum_copy(lax.rem(c + d, N), p).wait_send()
+                for piece in range(pieces):
+                    sum_copy(lax.rem(c + d, N), piece).wait_send()
 
         @pl.when(at_end)
         def _():
             for n in range(DEPTH):
-                slot = end_send.at[lax.rem(sent + parts - 1 + n, DEPTH)]
+                slot = end_send.at[lax.rem(sent + pieces - H + n, DEPTH)]
                 sum_copy(inner, 0, slot).wait_send()
 
 
@@ -470,9 +476,9 @@
             pltpu.VMEM((tokens, C), F32),
             pltpu.VMEM((cols, J, C), F32),
             pltpu.VMEM((R, chunks, cols, J, C), BF16),
-            pltpu.VMEM((N, parts, rows, J, C), F32),
-            pltpu.VMEM((N, parts, rows, J, C), BF16),
-            pltpu.VMEM((N, parts, rows, J, C), BF16),
+            pltpu.VMEM((N, parts * H, rows // H, J, C), F32),
+            pltpu.VMEM((N, parts * H, rows // H, J, C), BF16),
+            pltpu.VMEM((N, parts * H, rows // H, J, C), BF16),
         ]
         semaphores = [
             dma((9,)),
@@ -480,9 +486,9 @@
             dma((R // 2, chunks)),
             dma((R // 2, chunks)),
             dma((R, chunks)),
-            dma((N, parts)),
-            dma((N, parts)),
-            dma((N, parts)),
+            dma((N, parts * H)),
+            dma((N, parts * H)),
+            dma((N, parts * H)),
             dma((DEPTH,)),
         ]
         held = sum(math.prod(b.shape) * jnp.dtype(b.dtype).itemsize for b in buffers)

time: 30.6 us -> 30.4 us (level)
  the two profiles are of different devices: /device:TPU:24 before, /device:TPU:1 now
where the time goes in v4:
time: 30.4 us; the launch traced here: 30.2 us
  Pallas kernels  28.3 us (93%)
  other arithmetic  1.91 us (6%)
    pallas_call x1, Pallas kernels, per_device(): pl.pallas_call(functools.partial(kernel, R, N), out_shape=jax.ShapeDtypeS...  28.3 us
    add x1, other arithmetic, per_device(): return pair_rep + update  1.91 us

profile of v4, /device:TPU:1, one launch (start us, length us, event | category | flops | bytes accessed | tf_op | source)
XLA Modules:
  0.0 30.2 jit_solution(11595951410748245321)
XLA Ops:
  0.0 0.0 copy-start
  0.0 28.3 %shard_map.100 = f32[32,32,128]{2,1,0:T(8,128)} custom-call(f32[32,32,128]{2,1,0:T(8,128)} %pair_hbm.1, s32[1,128]{1,0:T(1,128)} %bitcast.7, s32[1,128]{1,0:T(1,128)} %bitcast.8, f32[1,128]{1,0:T(1,128)} %bitcast.9, f32[1,128]{1,0:T(1,128)} %bitcast.10, f32[1,128]{1,0:T(1,128)} %bitcast.11, bf16[128,640]{1,0:T(8,128)(2,1)} %w_in_hbm.1, f32[1,128]{1,0:T(1,128)} %bitcast.12, ...), custom_call_target="tpu_custom_call" | custom-call | tf_op jit(solution)/shard_map/pallas_call | solution.py:495
  28.3 0.0 copy-done
  28.3 1.9 %add.3 = f32[32,32,128]{2,1,0:T(8,128)} add(f32[32,32,128]{2,1,0:T(8,128)S(1)} %copy-done, f32[32,32,128]{2,1,0:T(8,128)} %shard_map.100) | non-fusion elementwise | flops 131072 | bytes 1572864 | tf_op jit(solution)/shard_map/add | solution.py:516
Async XLA Ops:
  0.0 28.3 %copy-start = (f32[32,32,128]{2,1,0:T(8,128)S(1)}, f32[32,32,128]{2,1,0:T(8,128)}, u32[]{:S(2)}) copy-start(f32[32,32,128]{2,1,0:T(8,128)} %pair_hbm.1) | copy-start | bytes 1572868
